TPU v7x, 512 devices: a whole 4x8x8 slice. The times are simulated.
512 devices in a mesh: grp: 8 (over y_lo, core), tile: 64 (over y_hi, x, z).
Axes of the slice: x: 4, y: 8 (y_hi: 2, y_lo: 4; y = y_hi * 4 + y_lo), z: 8, core: 2. Of those that a mesh axis runs over, the one named last changes fastest.
Arguments:
- hidden: bfloat16 [8, 512, 128, 128], P('grp', 'tile'), may hold values from -13 to 13
- cotangent: float32 [8, 512, 128], P('grp', 'tile'), may hold values from -16 to 16
- spectral_w: bfloat16 [4096, 256], P('tile'), may hold values from -0.375 to 0.375
- conv_k: float32 [9, 128], replicated, may hold values from -2 to 2
- proj_w: float32 [128], replicated, may hold values from -0.5 to 0.5
Outputs:
- grad_hidden: float32 [8, 512, 128, 128], P('grp', 'tile')
- grad_spectral: float32 [4096, 256], P('tile')
- grad_conv: float32 [9, 128], replicated
- grad_proj: float32 [128], replicated
All inputs are finite; a program needn't handle non-finite values.
Results may differ from a plain program's by a relative error of at most 0.015.
Values may be sent and summed in bfloat16 or wider, within the bound.
No kernel may reach another device: no remote copies, remote signals or barrier semaphores. Data moves between devices by JAX's collectives and lax.ppermute only.
A program may use at most 64 MiB of HBM per device.

v0:
```python
import jax
import jax.numpy as jnp
from jax import lax
from jax.sharding import PartitionSpec as P

HIGH = lax.Precision.HIGHEST


def padded(block, sides, width):
    for axis, dim in sides:
        count = lax.axis_size(axis)
        forward = [(i, i + 1) for i in range(count - 1)]
        backward = [(target, source) for source, target in forward]
        low = lax.ppermute(
            lax.slice_in_dim(block, block.shape[dim] - width, None, axis=dim), axis, forward
        )
        high = lax.ppermute(lax.slice_in_dim(block, 0, width, axis=dim), axis, backward)
        block = jnp.concatenate([low, block, high], axis=dim)
    return block


def spectral_tables(modes, bins):
    mode_idx = jnp.arange(modes, dtype=jnp.int32)
    bin_idx = jnp.arange(bins, dtype=jnp.int32)
    phase_int = mode_idx[:, None] * bin_idx[None, :] % bins
    angle_val = phase_int.astype(jnp.float32) * (2.0 * jnp.pi / bins)
    cosine = jnp.cos(angle_val)
    sine = jnp.sin(angle_val)
    forward_tab = jnp.concatenate([cosine, -sine], 0).astype(jnp.bfloat16)
    weight_k = jnp.where(mode_idx == 0, 1.0, 2.0).astype(jnp.float32)[:, None] / bins
    inverse_tab = jnp.concatenate([cosine * weight_k, -sine * weight_k], 0).T.astype(jnp.bfloat16)
    return (forward_tab, inverse_tab)


def build_mixer(weights, modes, chans):
    real_w = weights[:, :chans].reshape(modes, chans, chans)
    imag_w = weights[:, chans:].reshape(modes, chans, chans)
    upper = jnp.concatenate([real_w, imag_w], 2)
    lower = jnp.concatenate([-imag_w, real_w], 2)
    return jnp.concatenate([upper, lower], 1)


def gelu_pair(value):
    normal_cdf = 0.5 * (1.0 + jax.scipy.special.erf(value * 0.7071067811865476))
    return (
        value * normal_cdf,
        normal_cdf + value * jnp.exp(-0.5 * value * value) * 0.3989422804014327,
    )


def cell_backward(hidden_cells, local_term, cot_cells, mixer, forward_tab, inverse_tab, proj_w):
    modes = mixer.shape[0]
    chans = proj_w.shape[0]
    spec_h = jnp.einsum(
        "jb,pbc->jpc", forward_tab, hidden_cells, preferred_element_type=jnp.float32
    ).astype(jnp.bfloat16)
    h_cat = jnp.concatenate([spec_h[:modes], spec_h[modes:]], 2)
    mixed = jnp.einsum("kpa,kab->kpb", h_cat, mixer, preferred_element_type=jnp.float32).astype(
        jnp.bfloat16
    )
    mixed_stack = jnp.concatenate([mixed[:, :, :chans], mixed[:, :, chans:]], 0)
    spectral_out = jnp.einsum(
        "bj,jpo->pbo", inverse_tab, mixed_stack, preferred_element_type=jnp.float32
    )
    pre_act = spectral_out + local_term
    activ, slope = gelu_pair(pre_act)
    proj_grad = jnp.einsum("pb,pbo->o", cot_cells, activ, precision=HIGH)
    grad_pre = (cot_cells[:, :, None] * proj_w * slope).astype(jnp.bfloat16)
    grad_mix = jnp.einsum(
        "bj,pbo->jpo", inverse_tab, grad_pre, preferred_element_type=jnp.float32
    ).astype(jnp.bfloat16)
    grad_real = grad_mix[:modes]
    grad_imag = grad_mix[modes:]
    grad_cat = jnp.concatenate([grad_real, grad_imag], 2)
    grad_spec = jnp.einsum(
        "kpb,kab->kpa", grad_cat, mixer, preferred_element_type=jnp.float32
    ).astype(jnp.bfloat16)
    grad_stack = jnp.concatenate([grad_spec[:, :, :chans], grad_spec[:, :, chans:]], 0)
    grad_in = jnp.einsum("jb,jpc->pbc", forward_tab, grad_stack, preferred_element_type=jnp.float32)
    left_side = jnp.concatenate([spec_h[:modes], spec_h[modes:]], 1)
    right_side = jnp.concatenate([grad_cat, jnp.concatenate([grad_imag, -grad_real], 2)], 1)
    weight_term = jnp.einsum(
        "kpc,kpo->kco", left_side, right_side, preferred_element_type=jnp.float32
    ).reshape(modes * chans, 2 * chans)
    return (grad_pre, grad_in, weight_term, proj_grad)


def local(hidden, cotangent, spectral_w, conv_k, proj_w):
    rows_here, cols_here, bins_here, chans = hidden.shape
    modes = spectral_w.shape[0] * lax.axis_size("tile") // chans
    cell_count = rows_here * cols_here
    forward_tab, inverse_tab = spectral_tables(modes, bins_here)
    x_pad = padded(hidden, (("grp", 0), ("tile", 1)), 1)
    offsets = [(row_off, col_off) for row_off in (-1, 0, 1) for col_off in (-1, 0, 1)]
    local_term = jnp.zeros((rows_here, cols_here, bins_here, chans), jnp.float32)
    for index_d, (row_off, col_off) in enumerate(offsets):
        window = x_pad[1 + row_off : 1 + row_off + rows_here, 1 + col_off : 1 + col_off + cols_here]
        local_term = local_term + window.astype(jnp.float32) * conv_k[index_d]
    whole_w = lax.all_gather(spectral_w, "tile", axis=0, tiled=True)
    mixer = build_mixer(whole_w, modes, chans)
    grad_pre, grad_in, weight_term, proj_grad = cell_backward(
        hidden.reshape(cell_count, bins_here, chans),
        local_term.reshape(cell_count, bins_here, chans),
        cotangent.reshape(cell_count, bins_here),
        mixer,
        forward_tab,
        inverse_tab,
        proj_w,
    )
    grad_block = grad_pre.reshape(rows_here, cols_here, bins_here, chans)
    conv_part = jnp.stack(
        [
            jnp.einsum(
                "xybc,xybc->c",
                x_pad[1 + row_off : 1 + row_off + rows_here, 1 + col_off : 1 + col_off + cols_here],
                grad_block,
                preferred_element_type=jnp.float32,
            )
            for row_off, col_off in offsets
        ],
        0,
    )
    grad_pad = padded(grad_block, (("grp", 0), ("tile", 1)), 1)
    grad_hidden = grad_in.reshape(rows_here, cols_here, bins_here, chans)
    for index_d, (row_off, col_off) in enumerate(offsets):
        window = grad_pad[
            1 - row_off : 1 - row_off + rows_here, 1 - col_off : 1 - col_off + cols_here
        ]
        grad_hidden = grad_hidden + window.astype(jnp.float32) * conv_k[index_d]
    tile_share = lax.psum_scatter(weight_term, "tile", scatter_dimension=0, tiled=True)
    grad_spectral = lax.psum(tile_share.astype(jnp.bfloat16), "grp").astype(jnp.float32)
    conv_all, proj_all = lax.psum((conv_part, proj_grad), ("grp", "tile"))
    return (grad_hidden, grad_spectral, conv_all, proj_all)


def solution(mesh):
    in_specs = (P("grp", "tile", None, None), P("grp", "tile", None), P("tile", None), P(), P())
    out_specs = (P("grp", "tile", None, None), P("tile", None), P(), P())
    return jax.shard_map(local, mesh=mesh, in_specs=in_specs, out_specs=out_specs, check_vma=False)
```

profile of v0, /device:TPU:1, one launch (start us, length us, event | category | flops | bytes accessed | tf_op | source)
XLA Modules:
  0.0 639.4 jit_solution(11236863667525213482)
XLA Ops:
  7.9 1.1 copy.11
  9.1 8.8 %collective-permute-start.1 = (bf16[1,8,128,128]{2,3,1,0:T(8,128)(2,1)S(1)}, bf16[1,8,128,128]{2,3,1,0:T(8,128)(2,1)S(1)}, u32[]{:S(2)}, u32[]{:S(2)}) collective-permute-start(bf16[1,8,128,128]{2,3,1,0:T(8,128)(2,1)S(1)} %copy.11), channel_id=1, source_target_pairs={{64,0},{128,64},{192,128},{256,192},{320,256},{384,320},{448,384},... | collective-permute-start | bytes 786440 | tf_op jit(solution)/shard_map/ppermute | solution.py:17
  17.9 1.9 collective-permute-start
  19.9 1.1 convolution_convert_fusion.1
  21.1 1.0 slice_bitcast_fusion.8
  23.1 1.3 collective-permute-start.3
  24.4 4.0 collective-permute-start.2
  28.4 119.3 %all-gather.2.cloned.1.call-done = bf16[4096,256]{1,0:T(8,128)(2,1)} async-done(((bf16[64,256]{1,0:T(8,128)(2,1)}), bf16[4096,256]{1,0:T(8,128)(2,1)}) %all-gather.2.cloned.1.call-update) | async-done | bytes 2097168 | tf_op jit(solution)/shard_map/all_gather | solution.py:99
  147.7 1.7 fusion.52
  150.9 1.6 bitcast_convert_fusion
  152.8 2.7 fusion.24
  155.5 6.4 %collective-permute-start.5 = (bf16[1,8,128,128]{2,3,1,0:T(8,128)(2,1)S(1)}, bf16[1,8,128,128]{2,3,1,0:T(8,128)(2,1)}, u32[]{:S(2)}, u32[]{:S(2)}) collective-permute-start(bf16[1,8,128,128]{2,3,1,0:T(8,128)(2,1)S(1)} %bitcast.128), channel_id=1, source_target_pairs={{64,0},{128,64},{192,128},{256,192},{320,256},{384,320},{448,384},... | collective-permute-start | bytes 786440 | tf_op jit(solution)/shard_map/ppermute | solution.py:17
  161.9 5.1 collective-permute-start.4
  167.4 1.0 fusion.14
  168.4 1.2 fusion.15
  169.7 3.2 fusion.3
  173.5 97.4 %all-reduce = (f32[9,128]{1,0:T(8,128)}, f32[128]{0:T(128)}) all-reduce(f32[9,128]{1,0:T(8,128)S(1)} %stack.39, f32[128]{0:T(128)S(1)} %convolution_bitcast_fusion.2), channel_id=1, replica_groups=mesh['grp'=8,'tile'=64] {'grp','tile'}, use_global_device_ids=true, to_apply=%region_2.3 | all-reduce | flops 1280 | bytes 10240 | tf_op jit(solution)/shard_map/psum | solution.py:132
  271.8 1.3 collective-permute-start.6
  273.1 4.0 collective-permute-start.7
  277.5 1.3 collective-permute-done.7
  278.9 2.1 fusion.21
  281.1 1.0 copy.20
  282.1 273.8 %reduce-scatter.2.cloned.1.call-done = f32[64,256]{1,0:T(8,128)} async-done(((f32[4096,256]{1,0:T(8,128)}), f32[64,256]{1,0:T(8,128)}) %reduce-scatter.2.cloned.1.call-update) | async-done | bytes 65552 | tf_op jit(solution)/shard_map/reduce_scatter | solution.py:130
  556.7 75.3 %psum.21 = bf16[64,256]{1,0:T(8,128)(2,1)S(1)} all-reduce(bf16[64,256]{1,0:T(8,128)(2,1)S(1)} %convert_element_type.112), channel_id=1, replica_groups=mesh['grp'=8,'tile'=64] {'grp'}, use_global_device_ids=true, to_apply=%region_1.2 | all-reduce | flops 16384 | bytes 65536 | tf_op jit(solution)/shard_map/psum | solution.py:131
  (89 shorter events, 7.3 us)
Async XLA Ops:
  7.2 140.5 %all-gather.2.cloned.1.call-start = ((), (), s32[]{:S(2)}) async-start(), calls=%async_computation.1 | async-start | bytes 2129920 | tf_op jit(solution)/shard_map/all_gather | solution.py:99
  7.9 548.0 %reduce-scatter.2.cloned.1.call-start = ((), (), s32[]{:S(2)}) async-start(), calls=%async_computation.2 | async-start | bytes 4259840 | tf_op jit(solution)/shard_map/reduce_scatter | solution.py:130
  9.1 13.2 %collective-permute-start.1 = (bf16[1,8,128,128]{2,3,1,0:T(8,128)(2,1)S(1)}, bf16[1,8,128,128]{2,3,1,0:T(8,128)(2,1)S(1)}, u32[]{:S(2)}, u32[]{:S(2)}) collective-permute-start(bf16[1,8,128,128]{2,3,1,0:T(8,128)(2,1)S(1)} %copy.11), channel_id=1, source_target_pairs={{64,0},{128,64},{192,128},{256,192},{320,256},{384,320},{448,384},... | collective-permute-start | bytes 786440 | tf_op jit(solution)/shard_map/ppermute | solution.py:17
  17.9 5.2 collective-permute-start
  22.1 128.7 %copy-start.5 = (f32[128]{0:T(128)}, f32[128]{0:T(128)S(1)}, u32[]{:S(2)}) copy-start(f32[128]{0:T(128)S(1)} %get-tuple-element.35) | copy-start | bytes 1540
  22.1 128.7 %copy-start.7 = (f32[128]{0:T(128)}, f32[128]{0:T(128)S(1)}, u32[]{:S(2)}) copy-start(f32[128]{0:T(128)S(1)} %get-tuple-element.36) | copy-start | bytes 1540
  22.1 128.7 %copy-start.9 = (f32[128]{0:T(128)}, f32[128]{0:T(128)S(1)}, u32[]{:S(2)}) copy-start(f32[128]{0:T(128)S(1)} %get-tuple-element.37) | copy-start | bytes 1540
  22.1 128.7 %copy-start.11 = (f32[128]{0:T(128)}, f32[128]{0:T(128)S(1)}, u32[]{:S(2)}) copy-start(f32[128]{0:T(128)S(1)} %get-tuple-element.38) | copy-start | bytes 1540
  22.1 128.7 %copy-start.13 = (f32[128]{0:T(128)}, f32[128]{0:T(128)S(1)}, u32[]{:S(2)}) copy-start(f32[128]{0:T(128)S(1)} %get-tuple-element.39) | copy-start | bytes 1540
  22.1 128.7 %copy-start.15 = (f32[128]{0:T(128)}, f32[128]{0:T(128)S(1)}, u32[]{:S(2)}) copy-start(f32[128]{0:T(128)S(1)} %get-tuple-element.40) | copy-start | bytes 1540
  22.1 128.7 %copy-start.17 = (f32[128]{0:T(128)}, f32[128]{0:T(128)S(1)}, u32[]{:S(2)}) copy-start(f32[128]{0:T(128)S(1)} %get-tuple-element.41) | copy-start | bytes 1540
  22.1 128.7 %copy-start.19 = (f32[128]{0:T(128)}, f32[128]{0:T(128)S(1)}, u32[]{:S(2)}) copy-start(f32[128]{0:T(128)S(1)} %get-tuple-element.42) | copy-start | bytes 1540
  22.2 128.7 %copy-start.21 = (f32[128]{0:T(128)}, f32[128]{0:T(128)S(1)}, u32[]{:S(2)}) copy-start(f32[128]{0:T(128)S(1)} %get-tuple-element.43) | copy-start | bytes 1540
  23.1 127.7 %collective-permute-start.3 = (bf16[3,1,128,128]{2,3,1,0:T(8,128)(2,1)S(1)}, bf16[3,1,128,128]{2,3,1,0:T(8,128)(2,1)S(1)}, u32[]{:S(2)}, u32[]{:S(2)}) collective-permute-start(bf16[3,1,128,128]{2,3,1,0:T(8,128)(2,1)S(1)} %get-tuple-element.24), channel_id=1, source_target_pairs={{1,0},{2,1},{3,2},{4,3},{5,4},{6,5},{7,6},{8,7},{9,8},{10,9},{11,1... | collective-permute-start | bytes 294920 | tf_op jit(solution)/shard_map/ppermute | solution.py:17
  24.4 126.4 %collective-permute-start.2 = (bf16[3,1,128,128]{2,3,1,0:T(8,128)(2,1)S(1)}, bf16[3,1,128,128]{2,3,1,0:T(8,128)(2,1)S(1)}, u32[]{:S(2)}, u32[]{:S(2)}) collective-permute-start(bf16[3,1,128,128]{2,3,1,0:T(8,128)(2,1)S(1)} %get-tuple-element.25), channel_id=1, source_target_pairs={{0,1},{1,2},{2,3},{3,4},{4,5},{5,6},{6,7},{7,8},{8,9},{9,10},{10,1... | collective-permute-start | bytes 294920 | tf_op jit(solution)/shard_map/ppermute | solution.py:14
  155.5 115.4 %collective-permute-start.5 = (bf16[1,8,128,128]{2,3,1,0:T(8,128)(2,1)S(1)}, bf16[1,8,128,128]{2,3,1,0:T(8,128)(2,1)}, u32[]{:S(2)}, u32[]{:S(2)}) collective-permute-start(bf16[1,8,128,128]{2,3,1,0:T(8,128)(2,1)S(1)} %bitcast.128), channel_id=1, source_target_pairs={{64,0},{128,64},{192,128},{256,192},{320,256},{384,320},{448,384},... | collective-permute-start | bytes 786440 | tf_op jit(solution)/shard_map/ppermute | solution.py:17
  161.9 109.0 %collective-permute-start.4 = (bf16[1,8,128,128]{2,3,1,0:T(8,128)(2,1)S(1)}, bf16[1,8,128,128]{2,3,1,0:T(8,128)(2,1)}, u32[]{:S(2)}, u32[]{:S(2)}) collective-permute-start(bf16[1,8,128,128]{2,3,1,0:T(8,128)(2,1)S(1)} %bitcast.129), channel_id=1, source_target_pairs={{0,64},{64,128},{128,192},{192,256},{256,320},{320,384},{384,448},... | collective-permute-start | bytes 786440 | tf_op jit(solution)/shard_map/ppermute | solution.py:14
  169.6 109.2 %copy-start.6 = (f32[128]{0:T(128)S(1)}, f32[128]{0:T(128)}, u32[]{:S(2)}) copy-start(f32[128]{0:T(128)} %copy-done.5) | copy-start | bytes 1540
  169.6 109.2 %copy-start.8 = (f32[128]{0:T(128)S(1)}, f32[128]{0:T(128)}, u32[]{:S(2)}) copy-start(f32[128]{0:T(128)} %copy-done.7) | copy-start | bytes 1540
  169.6 109.2 %copy-start.10 = (f32[128]{0:T(128)S(1)}, f32[128]{0:T(128)}, u32[]{:S(2)}) copy-start(f32[128]{0:T(128)} %copy-done.9) | copy-start | bytes 1540
  169.6 109.2 %copy-start.12 = (f32[128]{0:T(128)S(1)}, f32[128]{0:T(128)}, u32[]{:S(2)}) copy-start(f32[128]{0:T(128)} %copy-done.11) | copy-start | bytes 1540
  169.7 109.2 %copy-start.14 = (f32[128]{0:T(128)S(1)}, f32[128]{0:T(128)}, u32[]{:S(2)}) copy-start(f32[128]{0:T(128)} %copy-done.13) | copy-start | bytes 1540
  271.8 5.8 collective-permute-start.6
  273.1 5.8 collective-permute-start.7
  (13 other events, 466.0 us)
Sparse Core Ops, SparseCore 0:
  12.6 135.0 all-gather.1
  155.6 400.1 reduce-scatter.1
where the time goes:
time: 640 us; the launch traced here: 639 us
  waiting for transfers between devices  396 us (62%)
  blocking collectives  173 us (27%)
  starting transfers between devices  32.8 us (5%)
  between operations  14.6 us (2%)
  matrix products  12.4 us (2%)
    reduce_scatter x1, waiting for transfers between devices, local(): lax.psum_scatter(weight_term, 'tile', scatter_dimension=0, tiled=True)  274 us
    all_gather x1, waiting for transfers between devices, local(): whole_w = lax.all_gather(spectral_w, 'tile', axis=0, tiled=True)  119 us
    psum x1, blocking collectives, local(): conv_all, proj_all = lax.psum((conv_part, proj_grad), ('grp', 'tile'))  97.4 us
    psum x1, blocking collectives, local(): lax.psum(tile_share.astype(jnp.bfloat16), 'grp').astype(jnp.float32)  75.3 us
    ppermute x4, starting transfers between devices, padded(): lax.ppermute(lax.slice_in_dim(block, 0, width, axis=dim), axis, backward)  17.8 us
    ppermute x4, starting transfers between devices, padded(): lax.ppermute(lax.slice_in_dim(block, block.shape[dim] - width, None, axis...  15 us
  transfers between devices with their start and end apart: 10, of which 5 were waited for; matrix products, arithmetic and copies ran while one was open for 3% of the time, Pallas kernels for 0%

commit v1 on v0

--- a/solution.py
+++ b/solution.py
@@ -96,7 +96,10 @@
     for index_d, (row_off, col_off) in enumerate(offsets):
         window = x_pad[1 + row_off : 1 + row_off + rows_here, 1 + col_off : 1 + col_off + cols_here]
         local_term = local_term + window.astype(jnp.float32) * conv_k[index_d]
-    whole_w = lax.all_gather(spectral_w, "tile", axis=0, tiled=True)
+    size = lax.axis_size("tile")
+    pieces = jnp.stack([spectral_w for _ in range(size)])
+    pieces = lax.all_to_all(pieces, "tile", split_axis=0, concat_axis=0)
+    whole_w = jnp.concatenate(pieces, axis=0)
     mixer = build_mixer(whole_w, modes, chans)
     grad_pre, grad_in, weight_term, proj_grad = cell_backward(
         hidden.reshape(cell_count, bins_here, chans),

time: 640 us -> 586 us (0.916)
  waiting for transfers between devices: 396 us -> 317 us
  blocking collectives: 173 us -> 184 us
  starting transfers between devices: 32.8 us -> 43.8 us
    all_gather x1 -> x0, waiting for transfers between devices: 119 us -> none  [local(): whole_w = lax.all_gather(spectral_w, 'tile', axis=0, tiled=True)]
    ppermute x4, waiting for transfers between devices: 0.45 us -> 44.1 us  [padded(): lax.ppermute(lax.slice_in_dim(block, 0, width, axis=dim), axis, backward)]
    all_to_all x0 -> x1, starting transfers between devices: none -> 19.6 us  [local(): pieces = lax.all_to_all(pieces, 'tile', split_axis=0, concat_axis=0)]
    psum x1, blocking collectives: 97.4 us -> 109 us  [local(): conv_all, proj_all = lax.psum((conv_part, proj_grad), ('grp', 'tile'))]
    ppermute x4, starting transfers between devices: 17.8 us -> 7.36 us  [padded(): lax.ppermute(lax.slice_in_dim(block, 0, width, axis=dim), axis, backward)]
  transfers between devices with their start and end apart: 10 -> 10, of which waited for: 5 -> 4; matrix products, arithmetic and copies ran while one was open for 3% -> 3% of each run, Pallas kernels for 0% -> 0%
where the time goes in v1:
time: 586 us; the launch traced here: 585 us
  waiting for transfers between devices  317 us (54%)
  blocking collectives  184 us (31%)
  starting transfers between devices  43.8 us (7%)
  between operations  14.7 us (3%)
  matrix products  12.4 us (2%)
  other arithmetic  7.31 us (1%)
    reduce_scatter x1, waiting for transfers between devices, local(): lax.psum_scatter(weight_term, 'tile', scatter_dimension=0, tiled=True)  272 us
    psum x1, blocking collectives, local(): conv_all, proj_all = lax.psum((conv_part, proj_grad), ('grp', 'tile'))  109 us
    psum x1, blocking collectives, local(): lax.psum(tile_share.astype(jnp.bfloat16), 'grp').astype(jnp.float32)  75.9 us
    ppermute x4, waiting for transfers between devices, padded(): lax.ppermute(lax.slice_in_dim(block, 0, width, axis=dim), axis, backward)  44.1 us
    all_to_all x1, starting transfers between devices, local(): pieces = lax.all_to_all(pieces, 'tile', split_axis=0, concat_axis=0)  19.6 us
    ppermute x4, starting transfers between devices, padded(): lax.ppermute(lax.slice_in_dim(block, block.shape[dim] - width, None, axis...  16.8 us
  transfers between devices with their start and end apart: 10, of which 4 were waited for; matrix products, arithmetic and copies ran while one was open for 3% of the time, Pallas kernels for 0%

profile of v1, /device:TPU:1, one launch (start us, length us, event | category | flops | bytes accessed | tf_op | source)
XLA Modules:
  0.0 585.1 jit_solution(6424242730201914376)
XLA Ops:
  7.2 2.4 stack.22
  9.6 19.6 %all-to-all-start = ((bf16[64,64,256]{2,1,0:T(8,128)(2,1)}), bf16[64,64,256]{2,1,0:T(8,128)(2,1)S(1)}, u32[]{:S(2)}, u32[]{:S(2)}) async-start(bf16[64,64,256]{2,1,0:T(8,128)(2,1)} %stack.22), calls=%async_computation | async-start | bytes 4194304 | tf_op jit(solution)/shard_map/all_to_all | solution.py:101
  29.4 2.9 collective-permute-start.1
  32.3 2.7 collective-permute-start
  37.3 43.7 %collective-permute-done.1 = bf16[1,8,128,128]{2,3,1,0:T(8,128)(2,1)S(1)} collective-permute-done((bf16[1,8,128,128]{2,3,1,0:T(8,128)(2,1)S(1)}, bf16[1,8,128,128]{2,3,1,0:T(8,128)(2,1)S(1)}, u32[]{:S(2)}, u32[]{:S(2)}) %collective-permute-start.1) | collective-permute-done | bytes 262176 | tf_op jit(solution)/shard_map/ppermute | solution.py:17
  81.8 1.3 collective-permute-start.3
  83.1 6.3 %collective-permute-start.2 = (bf16[3,1,128,128]{2,3,1,0:T(8,128)(2,1)}, bf16[3,1,128,128]{2,3,1,0:T(8,128)(2,1)}, u32[]{:S(2)}, u32[]{:S(2)}) collective-permute-start(bf16[3,1,128,128]{2,3,1,0:T(8,128)(2,1)} %get-tuple-element.25), channel_id=1, source_target_pairs={{0,1},{1,2},{2,3},{3,4},{4,5},{5,6},{6,7},{7,8},{8,9},{9,10},{10,1... | collective-permute-start | bytes 294920 | tf_op jit(solution)/shard_map/ppermute | solution.py:14
  90.0 0.9 fusion.2
  91.4 2.6 bitcast_convert_fusion
  94.4 2.7 fusion.24
  97.1 1.9 collective-permute-start.5
  99.0 3.9 collective-permute-start.4
  103.3 1.0 fusion.14
  104.3 1.2 fusion.15
  105.6 3.1 fusion.3
  109.4 108.6 %all-reduce = (f32[9,128]{1,0:T(8,128)}, f32[128]{0:T(128)}) all-reduce(f32[9,128]{1,0:T(8,128)S(1)} %stack.32, f32[128]{0:T(128)S(1)} %convolution_bitcast_fusion.2), channel_id=1, replica_groups=mesh['grp'=8,'tile'=64] {'grp','tile'}, use_global_device_ids=true, to_apply=%region_2.3 | all-reduce | flops 1280 | bytes 10240 | tf_op jit(solution)/shard_map/psum | solution.py:135
  218.8 1.3 collective-permute-start.6
  220.1 4.0 collective-permute-start.7
  224.6 1.2 collective-permute-done.7
  225.9 2.1 fusion.21
  227.9 1.0 copy.20
  228.9 271.9 %reduce-scatter.2.cloned.1.call-done = f32[64,256]{1,0:T(8,128)} async-done(((f32[4096,256]{1,0:T(8,128)}), f32[64,256]{1,0:T(8,128)}) %reduce-scatter.2.cloned.1.call-update) | async-done | bytes 65552 | tf_op jit(solution)/shard_map/reduce_scatter | solution.py:133
  500.9 0.8 convert_element_type.112
  501.7 75.9 %psum.21 = bf16[64,256]{1,0:T(8,128)(2,1)S(1)} all-reduce(bf16[64,256]{1,0:T(8,128)(2,1)S(1)} %convert_element_type.112), channel_id=1, replica_groups=mesh['grp'=8,'tile'=64] {'grp'}, use_global_device_ids=true, to_apply=%region_1.2 | all-reduce | flops 16384 | bytes 65536 | tf_op jit(solution)/shard_map/psum | solution.py:134
  (105 shorter events, 7.4 us)
Async XLA Ops:
  7.2 22.1 %copy-start = (bf16[1,8,128,128]{3,2,1,0:T(8,128)(2,1)S(1)}, bf16[1,8,128,128]{3,2,1,0:T(8,128)(2,1)}, u32[]{:S(2)}) copy-start(bf16[1,8,128,128]{3,2,1,0:T(8,128)(2,1)} %param.5) | copy-start | bytes 786436
  7.2 28.8 %copy-start.12 = (f32[9,128]{1,0:T(8,128)S(1)}, f32[9,128]{1,0:T(8,128)}, u32[]{:S(2)}) copy-start(f32[9,128]{1,0:T(8,128)} %param.8) | copy-start | bytes 13828
  9.6 79.8 %all-to-all-start = ((bf16[64,64,256]{2,1,0:T(8,128)(2,1)}), bf16[64,64,256]{2,1,0:T(8,128)(2,1)S(1)}, u32[]{:S(2)}, u32[]{:S(2)}) async-start(bf16[64,64,256]{2,1,0:T(8,128)(2,1)} %stack.22), calls=%async_computation | async-start | bytes 4194304 | tf_op jit(solution)/shard_map/all_to_all | solution.py:101
  29.2 471.7 %reduce-scatter.2.cloned.1.call-start = ((), (), s32[]{:S(2)}) async-start(), calls=%async_computation.2 | async-start | bytes 4259840 | tf_op jit(solution)/shard_map/reduce_scatter | solution.py:133
  29.4 51.6 %collective-permute-start.1 = (bf16[1,8,128,128]{2,3,1,0:T(8,128)(2,1)S(1)}, bf16[1,8,128,128]{2,3,1,0:T(8,128)(2,1)S(1)}, u32[]{:S(2)}, u32[]{:S(2)}) collective-permute-start(bf16[1,8,128,128]{2,3,1,0:T(8,128)(2,1)S(1)} %copy.11), channel_id=1, source_target_pairs={{64,0},{128,64},{192,128},{256,192},{320,256},{384,320},{448,384},... | collective-permute-start | bytes 786440 | tf_op jit(solution)/shard_map/ppermute | solution.py:17
  32.3 48.7 %collective-permute-start = (bf16[1,8,128,128]{2,3,1,0:T(8,128)(2,1)S(1)}, bf16[1,8,128,128]{2,3,1,0:T(8,128)(2,1)S(1)}, u32[]{:S(2)}, u32[]{:S(2)}) collective-permute-start(bf16[1,8,128,128]{2,3,1,0:T(8,128)(2,1)S(1)} %copy.11), channel_id=1, source_target_pairs={{0,64},{64,128},{128,192},{192,256},{256,320},{320,384},{384,448},... | collective-permute-start | bytes 786440 | tf_op jit(solution)/shard_map/ppermute | solution.py:14
  81.8 9.2 %collective-permute-start.3 = (bf16[3,1,128,128]{2,3,1,0:T(8,128)(2,1)}, bf16[3,1,128,128]{2,3,1,0:T(8,128)(2,1)}, u32[]{:S(2)}, u32[]{:S(2)}) collective-permute-start(bf16[3,1,128,128]{2,3,1,0:T(8,128)(2,1)} %get-tuple-element.24), channel_id=1, source_target_pairs={{1,0},{2,1},{3,2},{4,3},{5,4},{6,5},{7,6},{8,7},{9,8},{10,9},{11,1... | collective-permute-start | bytes 294920 | tf_op jit(solution)/shard_map/ppermute | solution.py:17
  83.1 7.9 %collective-permute-start.2 = (bf16[3,1,128,128]{2,3,1,0:T(8,128)(2,1)}, bf16[3,1,128,128]{2,3,1,0:T(8,128)(2,1)}, u32[]{:S(2)}, u32[]{:S(2)}) collective-permute-start(bf16[3,1,128,128]{2,3,1,0:T(8,128)(2,1)} %get-tuple-element.25), channel_id=1, source_target_pairs={{0,1},{1,2},{2,3},{3,4},{4,5},{5,6},{6,7},{7,8},{8,9},{9,10},{10,1... | collective-permute-start | bytes 294920 | tf_op jit(solution)/shard_map/ppermute | solution.py:14
  89.5 4.5 copy-start.7
  94.3 8.6 %copy-start.9 = (f32[128,128,8]{1,0,2:T(8,128)S(1)}, f32[128,128,8]{1,0,2:T(8,128)}, u32[]{:S(2)}) copy-start(f32[128,128,8]{1,0,2:T(8,128)} %get-tuple-element.18) | copy-start | bytes 1572868
  94.4 8.8 %copy-start.1 = (bf16[1,8,128,128]{3,2,1,0:T(8,128)(2,1)S(1)}, bf16[1,8,128,128]{3,2,1,0:T(8,128)(2,1)}, u32[]{:S(2)}) copy-start(bf16[1,8,128,128]{3,2,1,0:T(8,128)(2,1)} %param.5) | copy-start | bytes 786436
  97.1 120.9 %collective-permute-start.5 = (bf16[1,8,128,128]{2,3,1,0:T(8,128)(2,1)S(1)}, bf16[1,8,128,128]{2,3,1,0:T(8,128)(2,1)}, u32[]{:S(2)}, u32[]{:S(2)}) collective-permute-start(bf16[1,8,128,128]{2,3,1,0:T(8,128)(2,1)S(1)} %bitcast.130), channel_id=1, source_target_pairs={{64,0},{128,64},{192,128},{256,192},{320,256},{384,320},{448,384},... | collective-permute-start | bytes 786440 | tf_op jit(solution)/shard_map/ppermute | solution.py:17
  99.0 119.0 %collective-permute-start.4 = (bf16[1,8,128,128]{2,3,1,0:T(8,128)(2,1)S(1)}, bf16[1,8,128,128]{2,3,1,0:T(8,128)(2,1)}, u32[]{:S(2)}, u32[]{:S(2)}) collective-permute-start(bf16[1,8,128,128]{2,3,1,0:T(8,128)(2,1)S(1)} %bitcast.131), channel_id=1, source_target_pairs={{0,64},{64,128},{128,192},{192,256},{256,320},{320,384},{384,448},... | collective-permute-start | bytes 786440 | tf_op jit(solution)/shard_map/ppermute | solution.py:14
  105.5 120.3 %copy-start.14 = (f32[128]{0:T(128)S(1)}, f32[128]{0:T(128)}, u32[]{:S(2)}) copy-start(f32[128]{0:T(128)} %get-tuple-element.35) | copy-start | bytes 1540
  105.5 120.3 %copy-start.16 = (f32[128]{0:T(128)S(1)}, f32[128]{0:T(128)}, u32[]{:S(2)}) copy-start(f32[128]{0:T(128)} %get-tuple-element.36) | copy-start | bytes 1540
  105.5 120.3 %copy-start.18 = (f32[128]{0:T(128)S(1)}, f32[128]{0:T(128)}, u32[]{:S(2)}) copy-start(f32[128]{0:T(128)} %get-tuple-element.37) | copy-start | bytes 1540
  105.5 120.3 %copy-start.20 = (f32[128]{0:T(128)S(1)}, f32[128]{0:T(128)}, u32[]{:S(2)}) copy-start(f32[128]{0:T(128)} %get-tuple-element.38) | copy-start | bytes 1540
  105.5 120.3 %copy-start.22 = (f32[128]{0:T(128)S(1)}, f32[128]{0:T(128)}, u32[]{:S(2)}) copy-start(f32[128]{0:T(128)} %get-tuple-element.39) | copy-start | bytes 1540
  105.6 120.3 %copy-start.24 = (f32[128]{0:T(128)S(1)}, f32[128]{0:T(128)}, u32[]{:S(2)}) copy-start(f32[128]{0:T(128)} %get-tuple-element.40) | copy-start | bytes 1540
  105.6 120.3 %copy-start.26 = (f32[128]{0:T(128)S(1)}, f32[128]{0:T(128)}, u32[]{:S(2)}) copy-start(f32[128]{0:T(128)} %get-tuple-element.41) | copy-start | bytes 1540
  105.6 120.3 %copy-start.28 = (f32[128]{0:T(128)S(1)}, f32[128]{0:T(128)}, u32[]{:S(2)}) copy-start(f32[128]{0:T(128)} %get-tuple-element.42) | copy-start | bytes 1540
  105.6 120.3 %copy-start.30 = (f32[128]{0:T(128)S(1)}, f32[128]{0:T(128)}, u32[]{:S(2)}) copy-start(f32[128]{0:T(128)} %get-tuple-element.43) | copy-start | bytes 1540
  218.8 5.8 collective-permute-start.6
  220.1 5.7 collective-permute-start.7
  (21 other events, 38.5 us)
Sparse Core Ops, SparseCore 0:
  97.2 403.6 reduce-scatter.1
